TPU v7x, 128 devices: a whole 4x4x4 slice. The times are simulated.
128 devices in a mesh: enc: 4 (over z), region: 32 (over y, x, core).
Axes of the slice: x: 4, y: 4, z: 4, core: 2. Of those that a mesh axis runs over, the one named last changes fastest.
Arguments:
- embeddings: bfloat16 [131072, 1536], P(('enc', 'region')), may hold values from -6 to 6
- tile_position: int32 [131072], P(('enc', 'region')), may hold values from 0 to 131071, as said below
- w_in: bfloat16 [1536, 768], replicated, may hold values from -0.15625 to 0.15625
- ln_gain: bfloat16 [768], replicated, may hold values from 0.099609375 to 1.8984375
- w_query: bfloat16 [768, 768], replicated, may hold values from -0.14505926 to 0.14505926
- w_key: bfloat16 [768, 768], replicated, may hold values from -1.8222618 to 1.8222618
- w_value: bfloat16 [768, 768], replicated, may hold values from -0.21875 to 0.21875
- w_out: bfloat16 [768, 768], replicated, may hold values from -0.21875 to 0.21875
- near_lengths: int32 [4, 256], replicated, may hold values from 1 to 256, 32768 in all within a row
- far_lengths: int32 [4, 64], replicated, may hold values from 1 to 1024, 32768 in all within a row
- tissue: int32 [131072], P(('enc', 'region')), may hold values 0 or 1
- hospital: int32 [4], replicated, may hold values from 0 to 1, as said below
- w_kernel: float32 [768, 256], replicated, may hold values from -0.21875 to 0.21875
Outputs:
- features: bfloat16 [131072, 768], P(('enc', 'region'))
- statistic: float32 [], replicated
- kernel_grad: float32 [768, 256], replicated
Inputs may be any that keep to these rules, and one draw needn't show every extreme that they name: `tile_position`: every number of 0 to 131071 appears once; the 1024 rows of each device hold exactly 8 positions of each device's block of 1024 consecutive tile positions. `hospital`: each of the two labels is held by at least one of the 4 slides.
All inputs are finite; a program needn't handle non-finite values. No bound on the sum of `tissue` on one device may be relied on, other than what follows from the above.
Results may differ from a plain program's by a relative error of at most 0.012.
Values may be sent and summed in bfloat16 or wider, within the bound.
A program may use at most 128 MiB of HBM per device.

v0:
```python
import jax
import jax.numpy as jnp
from jax import lax
from jax.sharding import PartitionSpec as P

HEADS = 16
REGION = 256
DILATION = 4
NORM_EPSILON = 1e-05
MASKED_SCORE = -1e30
GRAD_SCALE = 100.0


def with_halo(x, sides, width):
    for axis, dim in sides:
        devices, length = (lax.axis_size(axis), x.shape[dim])
        up = [(i, (i + 1) % devices) for i in range(devices - 1)]
        down = [(j, i) for i, j in up]
        last = lax.slice_in_dim(x, length - width, length, axis=dim)
        initial = lax.slice_in_dim(x, 0, width, axis=dim)
        before = lax.ppermute(last, axis, up)
        after = lax.ppermute(initial, axis, down)
        x = jnp.concatenate([before, x, after], axis=dim)
    return x


def layer_norm(inputs):
    center = inputs - jnp.mean(inputs, axis=-1, keepdims=True)
    spread = jnp.mean(center * center, axis=-1, keepdims=True)
    return center * lax.rsqrt(spread + NORM_EPSILON)


def segment_ids(positions, lengths):
    segment_ends = jnp.cumsum(lengths, dtype=jnp.int32)
    passed = (segment_ends <= positions[..., None]).astype(jnp.int32)
    return jnp.sum(passed, axis=-1, dtype=jnp.int32)


def attend(queries, key_rows, values, key_pos, query_seg, key_seg, slide_len):
    scaling = queries.shape[-1] ** (-0.5)
    scores = (
        jnp.einsum("bqhe,bkhe->bhqk", queries, key_rows, preferred_element_type=jnp.float32)
        * scaling
    )
    allowed = (
        (query_seg[:, :, None] == key_seg[:, None, :])
        & (key_pos[:, None, :] >= 0)
        & (key_pos[:, None, :] < slide_len)
    )
    allowed = allowed[:, None, :, :]
    masked = jnp.where(allowed, scores, MASKED_SCORE)
    row_peak = jnp.max(masked, axis=-1, keepdims=True)
    exponent = jnp.where(allowed, jnp.exp(masked - row_peak), 0.0)
    row_total = jnp.sum(exponent, axis=-1, keepdims=True)
    weights = (exponent / row_total).astype(jnp.bfloat16)
    context = jnp.einsum("bhqk,bkhe->bqhe", weights, values, preferred_element_type=jnp.float32)
    return context.astype(jnp.bfloat16)


def block_context(queries, near_kv, far_kv, base_pos, near_row, far_row, slide_len):
    tile_rows, width = queries.shape
    half_width = width // 2
    head_count = HEADS // 2
    head_size = width // HEADS
    near_span = tile_rows // 4
    half_rows = tile_rows // 2
    steps_near = jnp.arange(tile_rows, dtype=jnp.int32)
    near_query = queries[:, :half_width].reshape(2, half_rows, head_count, head_size)
    near_keys = jnp.stack(
        [near_kv[0, :tile_rows], near_kv[0, half_rows : half_rows + tile_rows]]
    ).reshape(2, tile_rows, head_count, head_size)
    near_values = jnp.stack(
        [near_kv[1, :tile_rows], near_kv[1, half_rows : half_rows + tile_rows]]
    ).reshape(2, tile_rows, head_count, head_size)
    query_pos = base_pos + steps_near.reshape(2, half_rows)
    key_pos = base_pos - near_span + jnp.stack([steps_near, steps_near + half_rows])
    near_context = attend(
        near_query,
        near_keys,
        near_values,
        key_pos,
        segment_ids(query_pos, near_row),
        segment_ids(key_pos, near_row),
        slide_len,
    )
    near_context = near_context.reshape(tile_rows, half_width)
    group_rows = tile_rows // DILATION
    far_query = (
        queries[:, half_width:]
        .reshape(group_rows, DILATION, head_count, head_size)
        .transpose(1, 0, 2, 3)
    )
    far_keys = (
        far_kv[0].reshape(3 * group_rows, DILATION, head_count, head_size).transpose(1, 0, 2, 3)
    )
    far_values = (
        far_kv[1].reshape(3 * group_rows, DILATION, head_count, head_size).transpose(1, 0, 2, 3)
    )
    offsets = jnp.arange(DILATION, dtype=jnp.int32)[:, None]
    far_query_pos = base_pos + DILATION * jnp.arange(group_rows, dtype=jnp.int32)[None, :] + offsets
    far_key_pos = (
        base_pos
        - tile_rows
        + DILATION * jnp.arange(3 * group_rows, dtype=jnp.int32)[None, :]
        + offsets
    )
    far_context = attend(
        far_query,
        far_keys,
        far_values,
        far_key_pos,
        segment_ids(far_query_pos, far_row),
        segment_ids(far_key_pos, far_row),
        slide_len,
    )
    far_context = far_context.transpose(1, 0, 2, 3).reshape(tile_rows, half_width)
    return jnp.concatenate([near_context, far_context], axis=1)


def gaussian(left, right):
    left_sq = jnp.sum(left * left, axis=1)
    right_sq = jnp.sum(right * right, axis=1)
    inner = jnp.dot(left, right.T, precision=lax.Precision.HIGHEST)
    return jnp.exp(-(left_sq[:, None] + right_sq[None, :] - 2.0 * inner) / (2.0 * left.shape[1]))


def local(
    embeddings,
    tile_position,
    w_in,
    ln_gain,
    w_query,
    w_key,
    w_value,
    w_out,
    near_lengths,
    far_lengths,
    tissue,
    hospital,
    w_kernel,
):
    tile_rows = embeddings.shape[0]
    enc_count = lax.axis_size("enc")
    region_count = lax.axis_size("region")
    senders = enc_count * region_count
    per_peer = tile_rows // senders
    outgoing = jnp.argsort(tile_position)
    sorted_pos = tile_position[outgoing]
    payload = embeddings[outgoing]
    width_sent = payload.shape[1]
    arrived, arrived_pos = (
        lax.all_to_all(
            payload.reshape(senders, per_peer, width_sent),
            ("enc", "region"),
            split_axis=0,
            concat_axis=0,
            tiled=True,
        ),
        lax.all_to_all(
            sorted_pos.reshape(senders, per_peer),
            ("enc", "region"),
            split_axis=0,
            concat_axis=0,
            tiled=True,
        ),
    )
    placing = jnp.argsort(arrived_pos.reshape(tile_rows) % tile_rows)
    landed = arrived.reshape(tile_rows, width_sent)[placing]
    start_rows = jnp.dot(landed, w_in, preferred_element_type=jnp.float32).astype(jnp.bfloat16)
    normed = (layer_norm(start_rows.astype(jnp.float32)) * ln_gain.astype(jnp.float32)).astype(
        jnp.bfloat16
    )
    queries = jnp.dot(normed, w_query, preferred_element_type=jnp.float32).astype(jnp.bfloat16)
    d_model = queries.shape[1]
    half_width = d_model // 2
    near_span = tile_rows // 4
    base_pos = lax.axis_index("region") * tile_rows
    slide_len = tile_rows * region_count
    near_own = jnp.einsum(
        "rd,sdc->src",
        normed,
        jnp.stack([w_key[:, :half_width], w_value[:, :half_width]]),
        preferred_element_type=jnp.float32,
    ).astype(jnp.bfloat16)
    far_own = jnp.einsum(
        "rd,sdc->src",
        normed,
        jnp.stack([w_key[:, half_width:], w_value[:, half_width:]]),
        preferred_element_type=jnp.float32,
    ).astype(jnp.bfloat16)
    near_kv = with_halo(near_own, (("region", 1),), near_span)
    far_kv = with_halo(far_own, (("region", 1),), tile_rows)
    slide_index = lax.axis_index("enc")
    near_row = lax.dynamic_index_in_dim(near_lengths, slide_index, 0, keepdims=False)
    far_row = lax.dynamic_index_in_dim(far_lengths, slide_index, 0, keepdims=False)
    context = block_context(queries, near_kv, far_kv, base_pos, near_row, far_row, slide_len)
    features = (
        start_rows.astype(jnp.float32) + jnp.dot(context, w_out, preferred_element_type=jnp.float32)
    ).astype(jnp.bfloat16)
    reg_dev = tile_rows // REGION
    per_slide = reg_dev * region_count
    region_total = reg_dev * senders
    pooled = (
        jnp.einsum(
            "grd,gr->gd",
            features.reshape(reg_dev, REGION, d_model),
            tissue.reshape(reg_dev, REGION).astype(jnp.bfloat16),
            preferred_element_type=jnp.float32,
        )
        / REGION
    )
    normal_pool = layer_norm(pooled)
    slide_ids = jnp.arange(hospital.shape[0], dtype=jnp.int32)
    labelled_one = jnp.sum(hospital).astype(jnp.float32)
    count_one = labelled_one * per_slide
    count_zero = (hospital.shape[0] - labelled_one) * per_slide

    def region_weights(region_ids):
        owner_slide = region_ids // per_slide
        label_of = jnp.sum(
            jnp.where(owner_slide[:, None] == slide_ids[None, :], hospital[None, :], 0), axis=1
        )
        return jnp.where(label_of == 1, 1.0 / count_one, -1.0 / count_zero)

    embedded = jnp.dot(normal_pool, w_kernel, precision=lax.Precision.HIGHEST)
    device_pos = lax.axis_index("enc") * region_count + lax.axis_index("region")
    own_weights = region_weights(device_pos * reg_dev + jnp.arange(reg_dev, dtype=jnp.int32))
    piece = lax.all_gather(embedded, ("enc", "region"), axis=0, tiled=True)
    piece_ids = jnp.arange(piece.shape[0], dtype=jnp.int32)
    weighted = gaussian(embedded, piece) * region_weights(piece_ids)[None, :]
    kernel_sums = jnp.sum(weighted, axis=1)
    moments = jnp.dot(weighted, piece, precision=lax.Precision.HIGHEST)
    stat_part = region_total * jnp.sum(own_weights * kernel_sums)
    grad_embedded = (
        -2.0
        * region_total
        / embedded.shape[1]
        * own_weights[:, None]
        * (kernel_sums[:, None] * embedded - moments)
    )
    grad_part = GRAD_SCALE * jnp.dot(normal_pool.T, grad_embedded, precision=lax.Precision.HIGHEST)
    statistic, kernel_grad = lax.psum((stat_part, grad_part), ("enc", "region"))
    return (features, statistic, kernel_grad)


def solution(mesh):
    return jax.shard_map(
        local,
        mesh=mesh,
        in_specs=(
            P(("enc", "region"), None),
            P(("enc", "region")),
            P(),
            P(),
            P(),
            P(),
            P(),
            P(),
            P(),
            P(),
            P(("enc", "region")),
            P(),
            P(),
        ),
        out_specs=(P(("enc", "region"), None), P(), P()),
        check_vma=False,
    )
```

profile of v0, /device:TPU:1, one launch (start us, length us, event | category | flops | bytes accessed | tf_op | source)
XLA Modules:
  0.0 473.5 jit_solution(16803794036345877216)
XLA Ops:
  7.2 5.2 %sort.31 = (s32[1024]{0:T(1024)}, s32[1024]{0:T(1024)S(1)}) sort(s32[1024]{0:T(1024)} %param.14, s32[1024]{0:T(1024)S(1)} %iota.81), dimensions={0}, to_apply=%region_0.0 | sort | flops 10240 | bytes 16384 | tf_op jit(solution)/shard_map/jit(argsort)/sort | solution.py:147
  12.4 5.7 %gather_fusion.1 = s32[1024]{0:T(1024)S(1)} fusion(s32[1024]{0:T(1024)} %param.14, s32[1024]{0:T(1024)S(1)} %fusion.90), kind=kCustom, calls=%fused_computation.1 | custom fusion | bytes 12288 | tf_op jit(solution)/shard_map/gather | solution.py:148
  18.9 11.5 %all-to-all-start.1 = ((s32[128,1,8]{2,1,0:T(1,128)}), s32[128,1,8]{2,1,0:T(1,128)S(1)}, u32[]{:S(2)}, u32[]{:S(2)}) async-start(s32[128,1,8]{2,1,0:T(1,128)} %bitcast.2), calls=%async_computation.1 | async-start | bytes 131072 | tf_op jit(solution)/shard_map/all_to_all | solution.py:159
  30.4 2.5 fusion.111
  37.4 5.6 %gather_fusion = bf16[1024,1536]{1,0:T(8,128)(2,1)} fusion(bf16[1024,1536]{1,0:T(8,128)(2,1)S(1)} %copy-done, s32[1024]{0:T(1024)S(1)} %fusion.90), kind=kCustom, calls=%fused_computation | custom fusion | bytes 6295552 | tf_op jit(solution)/shard_map/gather | solution.py:149
  43.3 2.1 copy.77
  45.4 2.1 copy.76
  47.5 2.1 copy.75
  52.1 9.8 %all-to-all-start = ((bf16[128,8,1536]{2,1,0:T(8,128)(2,1)}), bf16[128,8,1536]{2,1,0:T(8,128)(2,1)S(1)}, u32[]{:S(2)}, u32[]{:S(2)}) async-start(bf16[128,8,1536]{2,1,0:T(8,128)(2,1)} %bitcast.105), calls=%async_computation | async-start | bytes 6291456 | tf_op jit(solution)/shard_map/all_to_all | solution.py:152
  64.6 1.6 and_and_fusion.1
  66.2 1.9 and_and_fusion
  69.5 4.4 sort.32
  73.9 29.5 %all-to-all-done = bf16[128,8,1536]{2,1,0:T(8,128)(2,1)S(1)} async-done(((bf16[128,8,1536]{2,1,0:T(8,128)(2,1)}), bf16[128,8,1536]{2,1,0:T(8,128)(2,1)S(1)}, u32[]{:S(2)}, u32[]{:S(2)}) %all-to-all-start) | async-done | bytes 3145760 | tf_op jit(solution)/shard_map/all_to_all | solution.py:152
  103.4 5.6 %gather_fusion.2 = bf16[1024,1536]{1,0:T(8,128)(2,1)} fusion(bf16[1024,1536]{1,0:T(8,128)(2,1)S(1)} %bitcast.104, s32[1024]{0:T(1024)S(1)} %fusion.91), kind=kCustom, calls=%fused_computation.2 | custom fusion | bytes 6295552 | tf_op jit(solution)/shard_map/gather | solution.py:168
  109.0 5.4 %convert_reduce_fusion = (f32[1024]{0:T(1024)S(1)}, bf16[1024,768]{1,0:T(8,128)(2,1)S(1)}) fusion(bf16[1024,1536]{1,0:T(8,128)(2,1)} %gather_fusion.2, bf16[1536,768]{1,0:T(8,128)(2,1)} %param.15), kind=kOutput, calls=%fused_computation.24 | convolution fusion | flops 2418277376 | bytes 7081984 | tf_op jit(solution)/shard_map/dot_general | solution.py:169
  115.1 2.7 fusion.46
  117.8 3.1 collective-permute-start.3
  120.9 2.5 collective-permute-start.2
  123.4 1.6 fusion.43
  125.9 3.0 collective-permute-start.1
  128.9 2.7 collective-permute-start
  131.6 1.5 convolution_convert_fusion.1
  134.3 3.1 reshape.336
  137.4 2.4 copy.67
  140.1 1.5 reshape.331
  141.6 2.4 collective-permute-done.1
  145.1 2.4 fusion.37
  147.6 22.4 %fusion.121 = (f32[2,8,512]{2,1,0:T(8,128)S(1)}, f32[2,8,512,1024]{3,2,1,0:T(8,128)}) fusion(bf16[2,1024,8,48]{1,3,2,0:T(8,128)(2,1)} %bitcast.109, pred[2,512,1024]{2,1,0:T(8,128)(4,1)} %and_and_fusion, bf16[2,512,8,48]{1,0,3,2:T(2,128)(2,1)} %reshape.331), kind=kOutput, calls=%fused_computation.160 | convolution fusion | flops 847250432 | bytes 36995072 | tf_op jit(solution)/shard_map/sub | solution.py:53
  169.9 13.5 %fusion.56 = bf16[2,512,8,48]{1,3,2,0:T(8,128)(2,1)S(1)} fusion(bf16[2,1024,8,48]{1,3,2,0:T(8,128)(2,1)S(1)} %bitcast.108, f32[2,8,512,1024]{3,2,1,0:T(8,128)} %get-tuple-element.30, f32[2,8,512]{2,1,0:T(8,128)S(1)} %get-tuple-element.29), kind=kOutput, calls=%fused_computation.67 | convolution fusion | flops 822476800 | bytes 35946496 | tf_op jit(solution)/shard_map/bhqk,bkhe->bqhe/dot_general | solution.py:56
  185.3 2.5 pad_maximum_fusion
  187.8 1.7 fusion.107
  189.5 4.3 copy.68
  193.8 9.3 %reshape_squeeze.7 = bf16[768,4,8,48]{3,2,1,0:T(8,128)(2,1)} reshape(bf16[1,3072,384]{2,1,0:T(8,128)(2,1)} %copy.68) | data formatting | bytes 4718592 | tf_op jit(solution)/shard_map/reshape;squeeze | solution.py:94
  203.1 7.9 %copy.69 = bf16[768,4,8,48]{0,3,2,1:T(8,128)(2,1)} copy(bf16[768,4,8,48]{3,2,1,0:T(8,128)(2,1)} %reshape_squeeze.7) | data formatting | bytes 4718592 | tf_op jit(solution)/shard_map/reshape;squeeze | solution.py:94
  211.0 2.6 copy.64
  213.6 9.3 %reshape_squeeze.6 = bf16[768,4,8,48]{3,2,1,0:T(8,128)(2,1)} reshape(bf16[1,3072,384]{2,1,0:T(8,128)(2,1)} %copy.64) | data formatting | bytes 4718592 | tf_op jit(solution)/shard_map/reshape;squeeze | solution.py:97
  222.9 8.1 %copy.65 = bf16[768,4,8,48]{0,3,2,1:T(8,128)(2,1)} copy(bf16[768,4,8,48]{3,2,1,0:T(8,128)(2,1)} %reshape_squeeze.6) | data formatting | bytes 4718592 | tf_op jit(solution)/shard_map/reshape;squeeze | solution.py:97
  230.9 16.9 %fusion.112 = (f32[4,8,256]{2,1,0:T(8,128)S(1)}, f32[4,8,256,768]{3,2,1,0:T(8,128)}) fusion(pred[4,256,768]{2,1,0:T(8,128)(4,1)S(1)} %copy-done.9, bf16[768,4,8,48]{0,3,2,1:T(8,128)(2,1)S(1)} %copy-done.5, bf16[256,4,8,48]{0,3,2,1:T(8,128)(2,1)} %copy.67), kind=kOutput, calls=%fused_computation.159 | convolution fusion | flops 635437824 | bytes 29130752 | tf_op jit(solution)/shard_map/sub | solution.py:53
  247.9 11.4 %fusion.53 = bf16[256,4,8,48]{0,3,2,1:T(8,128)(2,1)S(1)} fusion(f32[4,8,256,768]{3,2,1,0:T(8,128)} %get-tuple-element.28, f32[4,8,256]{2,1,0:T(8,128)S(1)} %get-tuple-element.27, bf16[768,4,8,48]{0,3,2,1:T(8,128)(2,1)} %copy.65), kind=kOutput, calls=%fused_computation.65 | convolution fusion | flops 616955904 | bytes 28344320 | tf_op jit(solution)/shard_map/bhqk,bkhe->bqhe/dot_general | solution.py:56
  259.3 3.0 copy.70
  264.9 3.7 fusion.19
  271.1 40.2 %all-gather = f32[128,4,256]{2,1,0:T(4,128)} all-gather(f32[1,4,256]{2,1,0:T(4,128)S(1)} %bitcast.115), channel_id=1, replica_groups=mesh['enc'=4,'region'=32] {'enc','region'}, dimensions={0}, use_global_device_ids=true | all-gather | bytes 528384 | tf_op jit(solution)/shard_map/all_gather | solution.py:228
  311.3 2.0 reshape.367
  314.5 1.7 fusion.126
  318.2 1.8 convolution_multiply_fusion
  320.6 64.7 %psum.14 = f32[]{:T(128)} all-reduce(f32[]{:T(128)S(6)} %mul.163), channel_id=1, replica_groups=mesh['enc'=4,'region'=32] {'enc','region'}, use_global_device_ids=true, to_apply=%region_24.25 | all-reduce | flops 1 | bytes 8 | tf_op jit(solution)/shard_map/psum | solution.py:242
  385.3 78.8 %all-reduce.2.cloned.1.call-done = f32[768,256]{1,0:T(8,128)} async-done(((f32[768,256]{1,0:T(8,128)}), f32[768,256]{1,0:T(8,128)}) %all-reduce.2.cloned.1.call-update) | async-done | bytes 786448 | tf_op jit(solution)/shard_map/psum | solution.py:242
  464.1 2.1 copy.107
  (113 shorter events, 25.2 us)
Async XLA Ops:
  7.2 30.2 %copy-start = (bf16[1024,1536]{1,0:T(8,128)(2,1)S(1)}, bf16[1024,1536]{1,0:T(8,128)(2,1)}, u32[]{:S(2)}) copy-start(bf16[1024,1536]{1,0:T(8,128)(2,1)} %param.13) | copy-start | bytes 9437188
  18.1 17.2 %copy-start.19 = (s32[4]{0:T(128)S(1)}, s32[4]{0:T(128)}, u32[]{:S(2)}) copy-start(s32[4]{0:T(128)} %param.24) | copy-start | bytes 52
  18.9 33.2 %all-to-all-start.1 = ((s32[128,1,8]{2,1,0:T(1,128)}), s32[128,1,8]{2,1,0:T(1,128)S(1)}, u32[]{:S(2)}, u32[]{:S(2)}) async-start(s32[128,1,8]{2,1,0:T(1,128)} %bitcast.2), calls=%async_computation.1 | async-start | bytes 131072 | tf_op jit(solution)/shard_map/all_to_all | solution.py:159
  30.4 2.5 copy-start.8
  37.4 10.1 %copy-start.18 = (bf16[768]{0:T(1024)(128)(2,1)S(1)}, bf16[768]{0:T(1024)(128)(2,1)}, u32[]{:S(2)}) copy-start(bf16[768]{0:T(1024)(128)(2,1)} %param.16) | copy-start | bytes 4612
  43.0 6.7 %copy-start.4 = (bf16[768,384]{1,0:T(8,128)(2,1)S(1)}, bf16[768,384]{1,0:T(8,128)(2,1)}, u32[]{:S(2)}) copy-start(bf16[768,384]{1,0:T(8,128)(2,1)} %get-tuple-element.17) | copy-start | bytes 1769476
  43.0 8.4 %copy-start.17 = (s32[1024]{0:T(1024)S(1)}, s32[1024]{0:T(1024)}, u32[]{:S(2)}) copy-start(s32[1024]{0:T(1024)} %param.23) | copy-start | bytes 12292
  52.1 51.3 %all-to-all-start = ((bf16[128,8,1536]{2,1,0:T(8,128)(2,1)}), bf16[128,8,1536]{2,1,0:T(8,128)(2,1)S(1)}, u32[]{:S(2)}, u32[]{:S(2)}) async-start(bf16[128,8,1536]{2,1,0:T(8,128)(2,1)} %bitcast.105), calls=%async_computation | async-start | bytes 6291456 | tf_op jit(solution)/shard_map/all_to_all | solution.py:152
  61.9 402.2 %all-reduce.2.cloned.1.call-start = ((), (), s32[]{:S(2)}) async-start(), calls=%async_computation.2 | async-start | bytes 1572864 | tf_op jit(solution)/shard_map/psum | solution.py:242
  109.0 6.0 %copy-start.13 = (bf16[768,384]{0,1:T(8,128)(2,1)S(1)}, bf16[768,384]{0,1:T(8,128)(2,1)}, u32[]{:S(2)}) copy-start(bf16[768,384]{0,1:T(8,128)(2,1)} %copy.77) | copy-start | bytes 1769476
  109.0 6.0 %copy-start.14 = (bf16[768,384]{0,1:T(8,128)(2,1)S(1)}, bf16[768,384]{0,1:T(8,128)(2,1)}, u32[]{:S(2)}) copy-start(bf16[768,384]{0,1:T(8,128)(2,1)} %copy.76) | copy-start | bytes 1769476
  114.4 17.2 %copy-start.6 = (bf16[1024,768]{1,0:T(8,128)(2,1)}, bf16[1024,768]{1,0:T(8,128)(2,1)S(1)}, u32[]{:S(2)}) copy-start(bf16[1024,768]{1,0:T(8,128)(2,1)S(1)} %get-tuple-element.26) | copy-start | bytes 4718596
  115.0 8.3 %copy-start.11 = (bf16[768,384]{0,1:T(8,128)(2,1)S(1)}, bf16[768,384]{0,1:T(8,128)(2,1)}, u32[]{:S(2)}) copy-start(bf16[768,384]{0,1:T(8,128)(2,1)} %copy.75) | copy-start | bytes 1769476
  115.1 8.3 %copy-start.12 = (bf16[768,384]{0,1:T(8,128)(2,1)S(1)}, bf16[768,384]{0,1:T(8,128)(2,1)}, u32[]{:S(2)}) copy-start(bf16[768,384]{0,1:T(8,128)(2,1)} %copy.74) | copy-start | bytes 1769476
  117.8 67.5 %collective-permute-start.3 = (bf16[2,1024,384]{1,2,0:T(8,128)(2,1)}, bf16[2,1024,384]{1,2,0:T(8,128)(2,1)}, u32[]{:S(2)}, u32[]{:S(2)}) collective-permute-start(bf16[2,1024,384]{1,2,0:T(8,128)(2,1)} %fusion.46), channel_id=1, source_target_pairs={{1,0},{2,1},{3,2},{4,3},{5,4},{6,5},{7,6},{8,7},{9,8},{10,9},{11,1... | collective-permute-start | bytes 4718600 | tf_op jit(solution)/shard_map/ppermute | solution.py:22
  120.9 64.4 %collective-permute-start.2 = (bf16[2,1024,384]{1,2,0:T(8,128)(2,1)}, bf16[2,1024,384]{1,2,0:T(8,128)(2,1)}, u32[]{:S(2)}, u32[]{:S(2)}) collective-permute-start(bf16[2,1024,384]{1,2,0:T(8,128)(2,1)} %fusion.46), channel_id=1, source_target_pairs={{0,1},{1,2},{2,3},{3,4},{4,5},{5,6},{6,7},{7,8},{8,9},{9,10},{10,1... | collective-permute-start | bytes 4718600 | tf_op jit(solution)/shard_map/ppermute | solution.py:21
  123.4 8.3 %copy-start.21 = (bf16[768,768]{1,0:T(8,128)(2,1)S(1)}, bf16[768,768]{1,0:T(8,128)(2,1)}, u32[]{:S(2)}) copy-start(bf16[768,768]{1,0:T(8,128)(2,1)} %param.17) | copy-start | bytes 3538948
  125.0 8.2 %copy-start.2 = (bf16[2,1024,384]{1,2,0:T(8,128)(2,1)}, bf16[2,1024,384]{1,2,0:T(8,128)(2,1)S(1)}, u32[]{:S(2)}) copy-start(bf16[2,1024,384]{1,2,0:T(8,128)(2,1)S(1)} %fusion.43) | copy-start | bytes 4718596
  125.9 18.2 %collective-permute-start.1 = (bf16[2,256,384]{1,2,0:T(8,128)(2,1)}, bf16[2,256,384]{1,2,0:T(8,128)(2,1)}, u32[]{:S(2)}, u32[]{:S(2)}) collective-permute-start(bf16[2,256,384]{1,2,0:T(8,128)(2,1)} %get-tuple-element.16), channel_id=1, source_target_pairs={{1,0},{2,1},{3,2},{4,3},{5,4},{6,5},{7,6},{8,7},{9,8},{10,9},{11,1... | collective-permute-start | bytes 1179656 | tf_op jit(solution)/shard_map/ppermute | solution.py:22
  128.9 16.2 %collective-permute-start = (bf16[2,256,384]{1,2,0:T(8,128)(2,1)S(1)}, bf16[2,256,384]{1,2,0:T(8,128)(2,1)}, u32[]{:S(2)}, u32[]{:S(2)}) collective-permute-start(bf16[2,256,384]{1,2,0:T(8,128)(2,1)S(1)} %get-tuple-element.15), channel_id=1, source_target_pairs={{0,1},{1,2},{2,3},{3,4},{4,5},{5,6},{6,7},{7,8},{8,9},{9,10},{10,1... | collective-permute-start | bytes 1179656 | tf_op jit(solution)/shard_map/ppermute | solution.py:21
  139.8 5.3 %copy-start.3 = (bf16[2,1024,384]{1,2,0:T(8,128)(2,1)S(1)}, bf16[2,1024,384]{1,2,0:T(8,128)(2,1)}, u32[]{:S(2)}) copy-start(bf16[2,1024,384]{1,2,0:T(8,128)(2,1)} %copy-done.2) | copy-start | bytes 4718596
  222.8 8.1 %copy-start.5 = (bf16[768,4,8,48]{0,3,2,1:T(8,128)(2,1)S(1)}, bf16[768,4,8,48]{0,3,2,1:T(8,128)(2,1)}, u32[]{:S(2)}) copy-start(bf16[768,4,8,48]{0,3,2,1:T(8,128)(2,1)} %copy.69) | copy-start | bytes 7077892
  222.9 8.1 %copy-start.9 = (pred[4,256,768]{2,1,0:T(8,128)(4,1)S(1)}, pred[4,256,768]{2,1,0:T(8,128)(4,1)}, u32[]{:S(2)}) copy-start(pred[4,256,768]{2,1,0:T(8,128)(4,1)} %and_and_fusion.1) | copy-start | bytes 2359300
  264.9 4.9 %copy-start.15 = (bf16[4,256,1]{1,2,0:T(2,128)(2,1)S(1)}, bf16[4,256,1]{1,2,0:T(2,128)(2,1)}, u32[]{:S(2)}) copy-start(bf16[4,256,1]{1,2,0:T(2,128)(2,1)} %reshape.372) | copy-start | bytes 6148
  264.9 5.5 %copy-start.10 = (f32[768,256]{1,0:T(8,128)S(1)}, f32[768,256]{1,0:T(8,128)}, u32[]{:S(2)}) copy-start(f32[768,256]{1,0:T(8,128)} %param.25) | copy-start | bytes 2359300
  268.7 1.1 copy-start.7
  268.7 45.8 %copy-start.16 = (f32[512]{0:T(512)S(1)}, f32[512]{0:T(512)}, u32[]{:S(2)}) copy-start(f32[512]{0:T(512)} %compare_select_fusion.2) | copy-start | bytes 6148
  268.7 47.5 %copy-start.20 = (s32[4]{0:T(128)S(1)}, s32[4]{0:T(128)}, u32[]{:S(2)}) copy-start(s32[4]{0:T(128)} %select_reduce_fusion.1) | copy-start | bytes 52
  271.1 195.1 %copy-start.1 = (bf16[1024,1536]{1,0:T(8,128)(2,1)S(1)}, bf16[1024,1536]{1,0:T(8,128)(2,1)}, u32[]{:S(2)}) copy-start(bf16[1024,1536]{1,0:T(8,128)(2,1)} %param.13) | copy-start | bytes 9437188
Sparse Core Ops, SparseCore 0:
  320.1 143.9 all-reduce.1
where the time goes:
time: 479 us; the launch traced here: 473 us
  waiting for transfers between devices  112 us (23%)
  blocking collectives  105 us (22%)
  local copies, waits for them, and re-layouts  96.9 us (20%)
  matrix products  84.8 us (18%)
  starting transfers between devices  33.1 us (7%)
  other arithmetic  25.6 us (5%)
  between operations  16.5 us (3%)
    psum x1, waiting for transfers between devices, local(): statistic, kernel_grad = lax.psum((stat_part, grad_part), ('enc', 'region'))  78.8 us
    psum x1, blocking collectives, local(): statistic, kernel_grad = lax.psum((stat_part, grad_part), ('enc', 'region'))  64.7 us
    all_gather x1, blocking collectives, local(): piece = lax.all_gather(embedded, ('enc', 'region'), axis=0, tiled=True)  40.2 us
    sub x2, matrix products, attend(): exponent = jnp.where(allowed, jnp.exp(masked - row_peak), 0.0)  39.3 us
    all_to_all x1, waiting for transfers between devices, local(): lax.all_to_all(payload.reshape(senders, per_peer, width_sent), ('enc', 'r...  29.5 us
    dot_general x2, matrix products, attend(): jnp.einsum('bhqk,bkhe->bqhe', weights, values, preferred_element_type=jnp...  24.8 us
    another operation x2, local copies, waits for them, and re-layouts, block_context(): far_kv[1].reshape(3 * group_rows, DILATION, head_count, head_size)  17.4 us
    another operation x2, local copies, waits for them, and re-layouts, block_context(): far_kv[0].reshape(3 * group_rows, DILATION, head_count, head_size)  17.2 us
  transfers between devices with their start and end apart: 7, of which 4 were waited for; matrix products, arithmetic and copies ran while one was open for 18% of the time, Pallas kernels for 0%

commit v1 on v0

--- a/solution.py
+++ b/solution.py
@@ -225,7 +225,12 @@
     embedded = jnp.dot(normal_pool, w_kernel, precision=lax.Precision.HIGHEST)
     device_pos = lax.axis_index("enc") * region_count + lax.axis_index("region")
     own_weights = region_weights(device_pos * reg_dev + jnp.arange(reg_dev, dtype=jnp.int32))
-    piece = lax.all_gather(embedded, ("enc", "region"), axis=0, tiled=True)
+    piece = jnp.concatenate(
+        lax.all_to_all(
+            jnp.stack([embedded] * lax.axis_size(("enc", "region"))), ("enc", "region"), 0, 0
+        ),
+        axis=0,
+    )
     piece_ids = jnp.arange(piece.shape[0], dtype=jnp.int32)
     weighted = gaussian(embedded, piece) * region_weights(piece_ids)[None, :]
     kernel_sums = jnp.sum(weighted, axis=1)

time: 479 us -> 461 us (0.962)
  blocking collectives: 105 us -> 62.6 us
  waiting for transfers between devices: 112 us -> 127 us
  starting transfers between devices: 33.1 us -> 41.5 us
    all_gather x1 -> x0, blocking collectives: 40.2 us -> none  [local(): piece = lax.all_gather(embedded, ('enc', 'region'), axis=0, tiled=True)]
    all_to_all x0 -> x1, waiting for transfers between devices: none -> 13 us  [local(): lax.all_to_all(jnp.stack([embedded] * lax.axis_size(('enc', 'region'))),...]
    all_to_all x0 -> x1, starting transfers between devices: none -> 8.31 us  [local(): lax.all_to_all(jnp.stack([embedded] * lax.axis_size(('enc', 'region'))),...]
    unnamed x51 -> x50, local copies, waits for them, and re-layouts: 13.8 us -> 11.8 us
  transfers between devices with their start and end apart: 7 -> 8, of which waited for: 4 -> 5; matrix products, arithmetic and copies ran while one was open for 18% -> 19% of each run, Pallas kernels for 0% -> 0%
where the time goes in v1:
time: 461 us; the launch traced here: 455 us
  waiting for transfers between devices  127 us (28%)
  local copies, waits for them, and re-layouts  98 us (21%)
  matrix products  84.8 us (18%)
  blocking collectives  62.6 us (14%)
  starting transfers between devices  41.5 us (9%)
  other arithmetic  25.1 us (5%)
  between operations  16.4 us (4%)
    psum x1, waiting for transfers between devices, local(): statistic, kernel_grad = lax.psum((stat_part, grad_part), ('enc', 'region'))  79.6 us
    psum x1, blocking collectives, local(): statistic, kernel_grad = lax.psum((stat_part, grad_part), ('enc', 'region'))  62.6 us
    sub x2, matrix products, attend(): exponent = jnp.where(allowed, jnp.exp(masked - row_peak), 0.0)  39.3 us
    all_to_all x1, waiting for transfers between devices, local(): lax.all_to_all(payload.reshape(senders, per_peer, width_sent), ('enc', 'r...  30.6 us
    dot_general x2, matrix products, attend(): jnp.einsum('bhqk,bkhe->bqhe', weights, values, preferred_element_type=jnp...  24.8 us
    another operation x2, local copies, waits for them, and re-layouts, block_context(): far_kv[1].reshape(3 * group_rows, DILATION, head_count, head_size)  17.4 us
    another operation x2, local copies, waits for them, and re-layouts, block_context(): far_kv[0].reshape(3 * group_rows, DILATION, head_count, head_size)  17.2 us
    all_to_all x1, waiting for transfers between devices, local(): lax.all_to_all(jnp.stack([embedded] * lax.axis_size(('enc', 'region'))),...  13 us
  transfers between devices with their start and end apart: 8, of which 5 were waited for; matrix products, arithmetic and copies ran while one was open for 19% of the time, Pallas kernels for 0%

profile of v1, /device:TPU:1, one launch (start us, length us, event | category | flops | bytes accessed | tf_op | source)
XLA Modules:
  0.0 455.2 jit_solution(452687411190350283)
XLA Ops:
  7.2 5.2 %sort.31 = (s32[1024]{0:T(1024)}, s32[1024]{0:T(1024)S(1)}) sort(s32[1024]{0:T(1024)} %param.14, s32[1024]{0:T(1024)S(1)} %iota.81), dimensions={0}, to_apply=%region_0.0 | sort | flops 10240 | bytes 16384 | tf_op jit(solution)/shard_map/jit(argsort)/sort | solution.py:147
  12.4 5.7 %gather_fusion.1 = s32[1024]{0:T(1024)S(1)} fusion(s32[1024]{0:T(1024)} %param.14, s32[1024]{0:T(1024)S(1)} %fusion.91), kind=kCustom, calls=%fused_computation.1 | custom fusion | bytes 12288 | tf_op jit(solution)/shard_map/gather | solution.py:148
  18.8 11.5 %all-to-all-start.1 = ((s32[128,1,8]{2,1,0:T(1,128)}), s32[128,1,8]{2,1,0:T(1,128)S(1)}, u32[]{:S(2)}, u32[]{:S(2)}) async-start(s32[128,1,8]{2,1,0:T(1,128)} %bitcast.2), calls=%async_computation.1 | async-start | bytes 131072 | tf_op jit(solution)/shard_map/all_to_all | solution.py:159
  31.0 2.5 fusion.112
  36.5 5.6 %gather_fusion = bf16[1024,1536]{1,0:T(8,128)(2,1)} fusion(bf16[1024,1536]{1,0:T(8,128)(2,1)S(1)} %copy-done, s32[1024]{0:T(1024)S(1)} %fusion.91), kind=kCustom, calls=%fused_computation | custom fusion | bytes 6295552 | tf_op jit(solution)/shard_map/gather | solution.py:149
  42.4 2.1 copy.133
  44.5 2.1 copy.132
  46.6 2.1 copy.131
  51.9 10.4 %all-to-all-start = ((bf16[128,8,1536]{2,1,0:T(8,128)(2,1)}), bf16[128,8,1536]{2,1,0:T(8,128)(2,1)S(1)}, u32[]{:S(2)}, u32[]{:S(2)}) async-start(bf16[128,8,1536]{2,1,0:T(8,128)(2,1)} %bitcast.104), calls=%async_computation | async-start | bytes 6291456 | tf_op jit(solution)/shard_map/all_to_all | solution.py:152
  63.8 1.6 and_and_fusion.1
  65.4 1.9 and_and_fusion
  68.8 4.4 sort.32
  73.2 30.6 %all-to-all-done = bf16[128,8,1536]{2,1,0:T(8,128)(2,1)S(1)} async-done(((bf16[128,8,1536]{2,1,0:T(8,128)(2,1)}), bf16[128,8,1536]{2,1,0:T(8,128)(2,1)S(1)}, u32[]{:S(2)}, u32[]{:S(2)}) %all-to-all-start) | async-done | bytes 3145760 | tf_op jit(solution)/shard_map/all_to_all | solution.py:152
  103.7 5.6 %gather_fusion.2 = bf16[1024,1536]{1,0:T(8,128)(2,1)} fusion(bf16[1024,1536]{1,0:T(8,128)(2,1)S(1)} %bitcast.103, s32[1024]{0:T(1024)S(1)} %fusion.92), kind=kCustom, calls=%fused_computation.2 | custom fusion | bytes 6295552 | tf_op jit(solution)/shard_map/gather | solution.py:168
  109.3 5.4 %convert_reduce_fusion = (f32[1024]{0:T(1024)S(1)}, bf16[1024,768]{1,0:T(8,128)(2,1)S(1)}) fusion(bf16[1024,1536]{1,0:T(8,128)(2,1)} %gather_fusion.2, bf16[1536,768]{1,0:T(8,128)(2,1)} %param.15), kind=kOutput, calls=%fused_computation.24 | convolution fusion | flops 2418277376 | bytes 7081984 | tf_op jit(solution)/shard_map/dot_general | solution.py:169
  115.4 2.7 fusion.46
  118.1 3.0 collective-permute-start.3
  121.1 2.5 collective-permute-start.2
  123.7 1.6 fusion.43
  126.2 3.0 collective-permute-start.1
  129.2 2.7 collective-permute-start
  132.0 1.5 convolution_convert_fusion.1
  134.6 3.1 reshape.343
  137.7 2.4 copy.120
  142.0 2.4 collective-permute-done.1
  145.4 2.4 fusion.37
  147.9 22.4 %fusion.122 = (f32[2,8,512]{2,1,0:T(8,128)S(1)}, f32[2,8,512,1024]{3,2,1,0:T(8,128)}) fusion(bf16[2,1024,8,48]{1,3,2,0:T(8,128)(2,1)} %bitcast.108, pred[2,512,1024]{2,1,0:T(8,128)(4,1)} %and_and_fusion, bf16[2,512,8,48]{1,0,3,2:T(2,128)(2,1)} %reshape.338), kind=kOutput, calls=%fused_computation.161 | convolution fusion | flops 847250432 | bytes 36995072 | tf_op jit(solution)/shard_map/sub | solution.py:53
  170.2 13.5 %fusion.56 = bf16[2,512,8,48]{1,3,2,0:T(8,128)(2,1)S(1)} fusion(bf16[2,1024,8,48]{1,3,2,0:T(8,128)(2,1)S(1)} %bitcast.107, f32[2,8,512,1024]{3,2,1,0:T(8,128)} %get-tuple-element.30, f32[2,8,512]{2,1,0:T(8,128)S(1)} %get-tuple-element.29), kind=kOutput, calls=%fused_computation.67 | convolution fusion | flops 822476800 | bytes 35946496 | tf_op jit(solution)/shard_map/bhqk,bkhe->bqhe/dot_general | solution.py:56
  185.6 2.5 pad_maximum_fusion
  188.1 1.7 fusion.108
  189.8 4.3 copy.121
  194.1 9.3 %reshape_squeeze.7 = bf16[768,4,8,48]{3,2,1,0:T(8,128)(2,1)} reshape(bf16[1,3072,384]{2,1,0:T(8,128)(2,1)} %copy.121) | data formatting | bytes 4718592 | tf_op jit(solution)/shard_map/reshape;squeeze | solution.py:94
  203.4 7.9 %copy.122 = bf16[768,4,8,48]{0,3,2,1:T(8,128)(2,1)} copy(bf16[768,4,8,48]{3,2,1,0:T(8,128)(2,1)} %reshape_squeeze.7) | data formatting | bytes 4718592 | tf_op jit(solution)/shard_map/reshape;squeeze | solution.py:94
  211.3 2.6 copy.117
  213.9 9.3 %reshape_squeeze.6 = bf16[768,4,8,48]{3,2,1,0:T(8,128)(2,1)} reshape(bf16[1,3072,384]{2,1,0:T(8,128)(2,1)} %copy.117) | data formatting | bytes 4718592 | tf_op jit(solution)/shard_map/reshape;squeeze | solution.py:97
  223.2 8.1 %copy.118 = bf16[768,4,8,48]{0,3,2,1:T(8,128)(2,1)} copy(bf16[768,4,8,48]{3,2,1,0:T(8,128)(2,1)} %reshape_squeeze.6) | data formatting | bytes 4718592 | tf_op jit(solution)/shard_map/reshape;squeeze | solution.py:97
  231.3 16.9 %fusion.113 = (f32[4,8,256]{2,1,0:T(8,128)S(1)}, f32[4,8,256,768]{3,2,1,0:T(8,128)}) fusion(pred[4,256,768]{2,1,0:T(8,128)(4,1)S(1)} %copy-done.9, bf16[768,4,8,48]{0,3,2,1:T(8,128)(2,1)S(1)} %copy-done.5, bf16[256,4,8,48]{0,3,2,1:T(8,128)(2,1)} %copy.120), kind=kOutput, calls=%fused_computation.160 | convolution fusion | flops 635437824 | bytes 29130752 | tf_op jit(solution)/shard_map/sub | solution.py:53
  248.2 11.4 %fusion.53 = bf16[256,4,8,48]{0,3,2,1:T(8,128)(2,1)S(1)} fusion(f32[4,8,256,768]{3,2,1,0:T(8,128)} %get-tuple-element.28, f32[4,8,256]{2,1,0:T(8,128)S(1)} %get-tuple-element.27, bf16[768,4,8,48]{0,3,2,1:T(8,128)(2,1)} %copy.118), kind=kOutput, calls=%fused_computation.65 | convolution fusion | flops 616955904 | bytes 28344320 | tf_op jit(solution)/shard_map/bhqk,bkhe->bqhe/dot_general | solution.py:56
  259.6 3.0 copy.123
  265.3 3.7 fusion.19
  272.2 8.3 %all-to-all-start.2 = ((f32[128,4,256]{2,1,0:T(4,128)}), f32[128,4,256]{2,1,0:T(4,128)}, u32[]{:S(2)}, u32[]{:S(2)}) async-start(f32[128,4,256]{2,1,0:T(4,128)} %stack.29), calls=%async_computation.2 | async-start | bytes 1048576 | tf_op jit(solution)/shard_map/all_to_all | solution.py:229
  280.9 13.0 %all-to-all-done.2 = f32[128,4,256]{2,1,0:T(4,128)} async-done(((f32[128,4,256]{2,1,0:T(4,128)}), f32[128,4,256]{2,1,0:T(4,128)}, u32[]{:S(2)}, u32[]{:S(2)}) %all-to-all-start.2) | async-done | bytes 524320 | tf_op jit(solution)/shard_map/all_to_all | solution.py:229
  295.4 2.0 reshape.346
  297.4 1.7 fusion.127
  301.0 1.8 convolution_multiply_fusion
  303.5 62.6 %psum.14 = f32[]{:T(128)} all-reduce(f32[]{:T(128)S(6)} %mul.164), channel_id=1, replica_groups=mesh['enc'=4,'region'=32] {'enc','region'}, use_global_device_ids=true, to_apply=%region_24.25 | all-reduce | flops 1 | bytes 8 | tf_op jit(solution)/shard_map/psum | solution.py:247
  366.1 79.6 %all-reduce.2.cloned.1.call-done = f32[768,256]{1,0:T(8,128)} async-done(((f32[768,256]{1,0:T(8,128)}), f32[768,256]{1,0:T(8,128)}) %all-reduce.2.cloned.1.call-update) | async-done | bytes 786448 | tf_op jit(solution)/shard_map/psum | solution.py:247
  445.8 2.1 copy.166
  (117 shorter events, 26.8 us)
Async XLA Ops:
  7.2 29.3 %copy-start = (bf16[1024,1536]{1,0:T(8,128)(2,1)S(1)}, bf16[1024,1536]{1,0:T(8,128)(2,1)}, u32[]{:S(2)}) copy-start(bf16[1024,1536]{1,0:T(8,128)(2,1)} %param.13) | copy-start | bytes 9437188
  18.8 33.0 %all-to-all-start.1 = ((s32[128,1,8]{2,1,0:T(1,128)}), s32[128,1,8]{2,1,0:T(1,128)S(1)}, u32[]{:S(2)}, u32[]{:S(2)}) async-start(s32[128,1,8]{2,1,0:T(1,128)} %bitcast.2), calls=%async_computation.1 | async-start | bytes 131072 | tf_op jit(solution)/shard_map/all_to_all | solution.py:159
  30.9 2.5 copy-start.8
  36.5 10.1 %copy-start.18 = (bf16[768]{0:T(1024)(128)(2,1)S(1)}, bf16[768]{0:T(1024)(128)(2,1)}, u32[]{:S(2)}) copy-start(bf16[768]{0:T(1024)(128)(2,1)} %param.16) | copy-start | bytes 4612
  42.1 6.7 %copy-start.4 = (bf16[768,384]{1,0:T(8,128)(2,1)S(1)}, bf16[768,384]{1,0:T(8,128)(2,1)}, u32[]{:S(2)}) copy-start(bf16[768,384]{1,0:T(8,128)(2,1)} %get-tuple-element.17) | copy-start | bytes 1769476
  42.1 7.8 %copy-start.19 = (s32[4]{0:T(128)S(1)}, s32[4]{0:T(128)}, u32[]{:S(2)}) copy-start(s32[4]{0:T(128)} %param.24) | copy-start | bytes 52
  42.1 9.1 %copy-start.17 = (s32[1024]{0:T(1024)S(1)}, s32[1024]{0:T(1024)}, u32[]{:S(2)}) copy-start(s32[1024]{0:T(1024)} %param.23) | copy-start | bytes 12292
  51.9 51.8 %all-to-all-start = ((bf16[128,8,1536]{2,1,0:T(8,128)(2,1)}), bf16[128,8,1536]{2,1,0:T(8,128)(2,1)S(1)}, u32[]{:S(2)}, u32[]{:S(2)}) async-start(bf16[128,8,1536]{2,1,0:T(8,128)(2,1)} %bitcast.104), calls=%async_computation | async-start | bytes 6291456 | tf_op jit(solution)/shard_map/all_to_all | solution.py:152
  109.3 6.0 %copy-start.13 = (bf16[768,384]{0,1:T(8,128)(2,1)S(1)}, bf16[768,384]{0,1:T(8,128)(2,1)}, u32[]{:S(2)}) copy-start(bf16[768,384]{0,1:T(8,128)(2,1)} %copy.133) | copy-start | bytes 1769476
  109.3 6.0 %copy-start.14 = (bf16[768,384]{0,1:T(8,128)(2,1)S(1)}, bf16[768,384]{0,1:T(8,128)(2,1)}, u32[]{:S(2)}) copy-start(bf16[768,384]{0,1:T(8,128)(2,1)} %copy.132) | copy-start | bytes 1769476
  114.7 17.2 %copy-start.6 = (bf16[1024,768]{1,0:T(8,128)(2,1)}, bf16[1024,768]{1,0:T(8,128)(2,1)S(1)}, u32[]{:S(2)}) copy-start(bf16[1024,768]{1,0:T(8,128)(2,1)S(1)} %get-tuple-element.26) | copy-start | bytes 4718596
  115.4 8.3 %copy-start.11 = (bf16[768,384]{0,1:T(8,128)(2,1)S(1)}, bf16[768,384]{0,1:T(8,128)(2,1)}, u32[]{:S(2)}) copy-start(bf16[768,384]{0,1:T(8,128)(2,1)} %copy.131) | copy-start | bytes 1769476
  115.4 8.3 %copy-start.12 = (bf16[768,384]{0,1:T(8,128)(2,1)S(1)}, bf16[768,384]{0,1:T(8,128)(2,1)}, u32[]{:S(2)}) copy-start(bf16[768,384]{0,1:T(8,128)(2,1)} %copy.130) | copy-start | bytes 1769476
  118.1 67.5 %collective-permute-start.3 = (bf16[2,1024,384]{1,2,0:T(8,128)(2,1)}, bf16[2,1024,384]{1,2,0:T(8,128)(2,1)}, u32[]{:S(2)}, u32[]{:S(2)}) collective-permute-start(bf16[2,1024,384]{1,2,0:T(8,128)(2,1)} %fusion.46), channel_id=1, source_target_pairs={{1,0},{2,1},{3,2},{4,3},{5,4},{6,5},{7,6},{8,7},{9,8},{10,9},{11,1... | collective-permute-start | bytes 4718600 | tf_op jit(solution)/shard_map/ppermute | solution.py:22
  121.1 64.4 %collective-permute-start.2 = (bf16[2,1024,384]{1,2,0:T(8,128)(2,1)}, bf16[2,1024,384]{1,2,0:T(8,128)(2,1)}, u32[]{:S(2)}, u32[]{:S(2)}) collective-permute-start(bf16[2,1024,384]{1,2,0:T(8,128)(2,1)} %fusion.46), channel_id=1, source_target_pairs={{0,1},{1,2},{2,3},{3,4},{4,5},{5,6},{6,7},{7,8},{8,9},{9,10},{10,1... | collective-permute-start | bytes 4718600 | tf_op jit(solution)/shard_map/ppermute | solution.py:21
  123.7 8.3 %copy-start.21 = (bf16[768,768]{1,0:T(8,128)(2,1)S(1)}, bf16[768,768]{1,0:T(8,128)(2,1)}, u32[]{:S(2)}) copy-start(bf16[768,768]{1,0:T(8,128)(2,1)} %param.17) | copy-start | bytes 3538948
  125.3 8.2 %copy-start.2 = (bf16[2,1024,384]{1,2,0:T(8,128)(2,1)}, bf16[2,1024,384]{1,2,0:T(8,128)(2,1)S(1)}, u32[]{:S(2)}) copy-start(bf16[2,1024,384]{1,2,0:T(8,128)(2,1)S(1)} %fusion.43) | copy-start | bytes 4718596
  126.2 18.2 %collective-permute-start.1 = (bf16[2,256,384]{1,2,0:T(8,128)(2,1)}, bf16[2,256,384]{1,2,0:T(8,128)(2,1)}, u32[]{:S(2)}, u32[]{:S(2)}) collective-permute-start(bf16[2,256,384]{1,2,0:T(8,128)(2,1)} %get-tuple-element.16), channel_id=1, source_target_pairs={{1,0},{2,1},{3,2},{4,3},{5,4},{6,5},{7,6},{8,7},{9,8},{10,9},{11,1... | collective-permute-start | bytes 1179656 | tf_op jit(solution)/shard_map/ppermute | solution.py:22
  129.2 16.2 %collective-permute-start = (bf16[2,256,384]{1,2,0:T(8,128)(2,1)S(1)}, bf16[2,256,384]{1,2,0:T(8,128)(2,1)}, u32[]{:S(2)}, u32[]{:S(2)}) collective-permute-start(bf16[2,256,384]{1,2,0:T(8,128)(2,1)S(1)} %get-tuple-element.15), channel_id=1, source_target_pairs={{0,1},{1,2},{2,3},{3,4},{4,5},{5,6},{6,7},{7,8},{8,9},{9,10},{10,1... | collective-permute-start | bytes 1179656 | tf_op jit(solution)/shard_map/ppermute | solution.py:21
  140.2 5.3 %copy-start.3 = (bf16[2,1024,384]{1,2,0:T(8,128)(2,1)S(1)}, bf16[2,1024,384]{1,2,0:T(8,128)(2,1)}, u32[]{:S(2)}) copy-start(bf16[2,1024,384]{1,2,0:T(8,128)(2,1)} %copy-done.2) | copy-start | bytes 4718596
  223.2 8.1 %copy-start.5 = (bf16[768,4,8,48]{0,3,2,1:T(8,128)(2,1)S(1)}, bf16[768,4,8,48]{0,3,2,1:T(8,128)(2,1)}, u32[]{:S(2)}) copy-start(bf16[768,4,8,48]{0,3,2,1:T(8,128)(2,1)} %copy.122) | copy-start | bytes 7077892
  223.2 8.1 %copy-start.9 = (pred[4,256,768]{2,1,0:T(8,128)(4,1)S(1)}, pred[4,256,768]{2,1,0:T(8,128)(4,1)}, u32[]{:S(2)}) copy-start(pred[4,256,768]{2,1,0:T(8,128)(4,1)} %and_and_fusion.1) | copy-start | bytes 2359300
  265.2 4.9 %copy-start.15 = (bf16[4,256,1]{1,2,0:T(2,128)(2,1)S(1)}, bf16[4,256,1]{1,2,0:T(2,128)(2,1)}, u32[]{:S(2)}) copy-start(bf16[4,256,1]{1,2,0:T(2,128)(2,1)} %reshape.378) | copy-start | bytes 6148
  265.3 5.5 %copy-start.10 = (f32[768,256]{1,0:T(8,128)S(1)}, f32[768,256]{1,0:T(8,128)}, u32[]{:S(2)}) copy-start(f32[768,256]{1,0:T(8,128)} %param.25) | copy-start | bytes 2359300
  269.0 1.1 copy-start.7
  269.0 11.6 %copy-start.20 = (s32[4]{0:T(128)S(1)}, s32[4]{0:T(128)}, u32[]{:S(2)}) copy-start(s32[4]{0:T(128)} %param.24) | copy-start | bytes 52
  269.0 11.8 %copy-start.16 = (s32[512]{0:T(512)S(1)}, s32[512]{0:T(512)}, u32[]{:S(2)}) copy-start(s32[512]{0:T(512)} %add_select_fusion.1) | copy-start | bytes 6148
  272.2 21.7 %all-to-all-start.2 = ((f32[128,4,256]{2,1,0:T(4,128)}), f32[128,4,256]{2,1,0:T(4,128)}, u32[]{:S(2)}, u32[]{:S(2)}) async-start(f32[128,4,256]{2,1,0:T(4,128)} %stack.29), calls=%async_computation.2 | async-start | bytes 1048576 | tf_op jit(solution)/shard_map/all_to_all | solution.py:229
  280.6 167.3 %copy-start.1 = (bf16[1024,1536]{1,0:T(8,128)(2,1)S(1)}, bf16[1024,1536]{1,0:T(8,128)(2,1)}, u32[]{:S(2)}) copy-start(bf16[1024,1536]{1,0:T(8,128)(2,1)} %param.13) | copy-start | bytes 9437188
  280.6 165.2 %all-reduce.2.cloned.1.call-start = ((), (), s32[]{:S(2)}) async-start(), calls=%async_computation.3 | async-start | bytes 1572864 | tf_op jit(solution)/shard_map/psum | solution.py:247
Sparse Core Ops, SparseCore 0:
  303.0 142.7 all-reduce.1
